TPU v7x, 32 devices: a whole 2x2x4 slice. The times are simulated.
32 devices in a mesh: groups: 2 (over x), ctx: 16 (over z, y, core).
Axes of the slice: x: 2, y: 2, z: 4, core: 2. Of those that a mesh axis runs over, the one named last changes fastest.
Arguments:
- hidden: bfloat16 [4096, 4096], P(('groups', 'ctx')), parts along dimension 0, may hold values from -6 to 6
- frozen_query: bfloat16 [4096, 2048], P(('groups', 'ctx')), parts along dimension 0, may hold values from -18 to 18
- frozen_key: bfloat16 [4096, 512], P(('groups', 'ctx')), parts along dimension 0, may hold values from -18 to 18
- frozen_value: bfloat16 [4096, 512], P(('groups', 'ctx')), parts along dimension 0, may hold values from -6 to 6
- adapter_bank: bfloat16 [16, 64, 21504], P('ctx'), may hold values from -0.57 to 0.57
- request_shards: int32 [6], P('groups'), parts along dimension 0, may hold values from 1 to 9, 16 in all
- request_adapter: int32 [6], P('groups'), parts along dimension 0, may hold values from 0 to 15
- adapter_owner: int32 [16], replicated, may hold values from 0 to 15, each once
Outputs:
- attention: bfloat16 [4096, 2048], P(('groups', 'ctx')), parts along dimension 0
- adapter_output: bfloat16 [4096, 4096], P(('groups', 'ctx')), parts along dimension 0
There are 2 independent parts, one for each index of `groups`. A program takes and returns all parts, laid end to end along the dimension named above; an argument that names none is the same for every part. Nothing has to cross between parts.
Inputs may be any that keep to these rules, and one draw needn't show every extreme that they name: `request_shards`: request lengths sum to 16; the longest has exactly 9 shards. `adapter_owner`: a permutation: every bank entry holds exactly one adapter.
All inputs are finite; a program needn't handle non-finite values.
Results may differ from a plain program's by a relative error of at most 0.012.
Values may be sent and summed in bfloat16 or wider, within the bound.
No kernel may reach another device: no remote copies, remote signals or barrier semaphores. Data moves between devices by JAX's collectives and lax.ppermute only.
A program may use at most 64 MiB of HBM per device.

v0:
```python
import jax
import jax.numpy as jnp
from jax import lax
from jax.sharding import PartitionSpec as P

HEAD_SIZE = 128
QUERY_HEADS = 16
KEY_VALUE_HEADS = 4


adapter_scale = 0.5
rope_theta = 500000.0
score_masked = -1e30


def shifted(block, axis, distance):
    devices = range(lax.axis_size(axis))
    route = [((i - distance) % len(devices), i) for i in devices]
    return lax.ppermute(block, axis, route)


def request_layout(request_shards, shards):
    starts = jnp.cumsum(request_shards) - request_shards
    shard_ids = jnp.arange(shards, dtype=jnp.int32)
    request_of = jnp.sum((starts[None, :] <= shard_ids[:, None]).astype(jnp.int32), axis=1) - 1
    longest = jnp.argmax(request_shards)
    offset = (starts[longest] + request_shards[longest] // 2) % shards
    packed_of = (shard_ids + offset) % shards
    return (request_of, starts, packed_of)


def rotate(value_matrix, positions):
    half_dim = HEAD_SIZE // 2
    frequency = rope_theta ** (-(jnp.arange(half_dim, dtype=jnp.float32) * 2.0) / HEAD_SIZE)
    angles = positions.astype(jnp.float32)[:, None] * frequency[None, :]
    cosines = jnp.concatenate([jnp.cos(angles), jnp.cos(angles)], 1)[:, None, :]
    sines = jnp.concatenate([jnp.sin(angles), jnp.sin(angles)], 1)[:, None, :]
    front_half = value_matrix[..., :half_dim]
    second = value_matrix[..., half_dim:]
    turned = jnp.concatenate([-second, front_half], -1)
    return value_matrix * cosines + turned * sines


def project(hidden, frozen_query, frozen_key, frozen_value, adapter, positions):
    model_width = hidden.shape[1]
    query_width = frozen_query.shape[1]
    key_width = frozen_key.shape[1]
    token_rows = hidden.shape[0]
    low_parts = []
    for which in range(3):
        down_cols = adapter[:, which * model_width : (which + 1) * model_width]
        low_parts.append(
            jnp.dot(hidden, down_cols.T, preferred_element_type=jnp.float32).astype(jnp.bfloat16)
        )
    upward_columns = adapter[:, 3 * model_width : 3 * model_width + query_width + 2 * key_width]
    query_update = jnp.dot(
        low_parts[0], upward_columns[:, :query_width], preferred_element_type=jnp.float32
    )
    key_update = jnp.dot(
        low_parts[1],
        upward_columns[:, query_width : query_width + key_width],
        preferred_element_type=jnp.float32,
    )
    value_update = jnp.dot(
        low_parts[2],
        upward_columns[:, query_width + key_width :],
        preferred_element_type=jnp.float32,
    )
    query_matrix = frozen_query.astype(jnp.float32) + adapter_scale * query_update
    key_output = frozen_key.astype(jnp.float32) + adapter_scale * key_update
    value_output = (frozen_value.astype(jnp.float32) + adapter_scale * value_update).astype(
        jnp.bfloat16
    )
    query_matrix = rotate(
        query_matrix.reshape(token_rows, query_width // HEAD_SIZE, HEAD_SIZE), positions
    ).reshape(token_rows, query_width)
    key_output = rotate(
        key_output.reshape(token_rows, key_width // HEAD_SIZE, HEAD_SIZE), positions
    ).reshape(token_rows, key_width)
    return (query_matrix.astype(jnp.bfloat16), key_output.astype(jnp.bfloat16), value_output)


def output_adapter(attended_output, adapter, model_width):
    query_width = attended_output.shape[1]
    bank_width = adapter.shape[1]
    down_cols = adapter[:, bank_width - model_width - query_width : bank_width - model_width]
    upward_columns = adapter[:, bank_width - model_width :]
    reduced_rank = jnp.dot(attended_output, down_cols.T, preferred_element_type=jnp.float32).astype(
        jnp.bfloat16
    )
    return (
        adapter_scale * jnp.dot(reduced_rank, upward_columns, preferred_element_type=jnp.float32)
    ).astype(jnp.bfloat16)


def body(
    hidden,
    frozen_query,
    frozen_key,
    frozen_value,
    adapter_bank,
    request_shards,
    request_adapter,
    adapter_owner,
):
    shards = lax.axis_size("ctx")
    own_index = lax.axis_index("ctx")
    token_rows = hidden.shape[0]
    request_of, starts, packed_of = request_layout(request_shards, shards)
    own_packed = packed_of[own_index]
    own_request = request_of[own_packed]
    query_index = own_packed * token_rows + jnp.arange(token_rows, dtype=jnp.int32)
    positions = query_index - starts[own_request] * token_rows
    own_adapter = adapter_bank[0]
    rank_rows = own_adapter.shape[0]
    pieces = own_adapter.reshape(shards, rank_rows // shards, own_adapter.shape[1])
    rank_slices = lax.all_to_all(pieces, "ctx", split_axis=0, concat_axis=0, tiled=True)
    wanted = adapter_owner[request_adapter[request_of[packed_of]]]
    outgoing = jnp.take(rank_slices, wanted, axis=0)
    adapter = lax.all_to_all(outgoing, "ctx", split_axis=0, concat_axis=1, tiled=True)[0]
    query_matrix, key_output, value_output = project(
        hidden, frozen_query, frozen_key, frozen_value, adapter, positions
    )
    group_split = QUERY_HEADS // KEY_VALUE_HEADS
    head_groups = (
        query_matrix.reshape(token_rows, KEY_VALUE_HEADS, group_split, HEAD_SIZE)
        .transpose(1, 2, 0, 3)
        .reshape(KEY_VALUE_HEADS, group_split * token_rows, HEAD_SIZE)
    )
    paired_key_value = jnp.stack([key_output, value_output])
    inverse_root = 1.0 / jnp.sqrt(jnp.float32(HEAD_SIZE))
    running = (
        jnp.full((KEY_VALUE_HEADS, group_split * token_rows), score_masked, jnp.float32),
        jnp.zeros((KEY_VALUE_HEADS, group_split * token_rows), jnp.float32),
        jnp.zeros((KEY_VALUE_HEADS, group_split * token_rows, HEAD_SIZE), jnp.float32),
    )

    def attend(running, paired_key_value, source):
        source_packed = packed_of[source]
        same_request = request_of[source_packed] == own_request
        best_score, softmax_total, weighted_values = running
        key_block = paired_key_value[0].reshape(token_rows, KEY_VALUE_HEADS, HEAD_SIZE)
        value_block = paired_key_value[1].reshape(token_rows, KEY_VALUE_HEADS, HEAD_SIZE)
        score_matrix = (
            jnp.einsum("jqv,wjv->jqw", head_groups, key_block, preferred_element_type=jnp.float32)
            * inverse_root
        )
        key_index = source_packed * token_rows + jnp.arange(token_rows, dtype=jnp.int32)
        allowed = same_request & (key_index[None, :] <= query_index[:, None])
        allowed = jnp.tile(allowed, (group_split, 1))
        score_matrix = jnp.where(allowed[None], score_matrix, score_masked)
        new_best = jnp.maximum(best_score, jnp.max(score_matrix, axis=-1))
        shrink = jnp.exp(best_score - new_best)
        attention_weight = jnp.exp(score_matrix - new_best[..., None])
        softmax_total = softmax_total * shrink + jnp.sum(attention_weight, axis=-1)
        weighted_values = weighted_values * shrink[..., None] + jnp.einsum(
            "vel,lvw->vew",
            attention_weight.astype(jnp.bfloat16),
            value_block,
            preferred_element_type=jnp.float32,
        )
        return (new_best, softmax_total, weighted_values)

    running = attend(running, paired_key_value, own_index)

    def advance(turn_index, carried):
        running, paired_key_value = carried
        paired_key_value = shifted(paired_key_value, "ctx", 1)
        source = (own_index - turn_index) % shards
        return (attend(running, paired_key_value, source), paired_key_value)

    running, paired_key_value = lax.fori_loop(1, shards, advance, (running, paired_key_value))
    best_score, softmax_total, weighted_values = running
    attended_output = (weighted_values / softmax_total[..., None]).reshape(
        KEY_VALUE_HEADS, group_split, token_rows, HEAD_SIZE
    )
    attended_output = (
        attended_output.transpose(2, 0, 1, 3)
        .reshape(token_rows, KEY_VALUE_HEADS * group_split * HEAD_SIZE)
        .astype(jnp.bfloat16)
    )
    return (attended_output, output_adapter(attended_output, adapter, hidden.shape[1]))


def solution(mesh):
    return jax.shard_map(
        body,
        mesh=mesh,
        in_specs=(
            P(("groups", "ctx"), None),
            P(("groups", "ctx"), None),
            P(("groups", "ctx"), None),
            P(("groups", "ctx"), None),
            P("ctx", None, None),
            P("groups"),
            P("groups"),
            P(),
        ),
        out_specs=(P(("groups", "ctx"), None), P(("groups", "ctx"), None)),
        check_vma=False,
    )
```

profile of v0, /device:TPU:0, one launch (start us, length us, event | category | flops | bytes accessed | tf_op | source)
XLA Modules:
  0.0 320.1 jit_solution(4403329119307172989)
XLA Ops:
  0.6 4.5 %reshape_squeeze.3 = bf16[16,4,21504]{2,1,0:T(4,128)(2,1)} reshape(bf16[1,64,21504]{2,1,0:T(8,128)(2,1)} %param.14) | data formatting | bytes 5505024 | tf_op jit(solution)/shard_map/reshape;squeeze | solution.py:116
  5.2 7.6 %all-to-all-start = ((bf16[16,4,21504]{2,1,0:T(4,128)(2,1)}), bf16[16,4,21504]{2,1,0:T(4,128)(2,1)}, u32[]{:S(2)}, u32[]{:S(2)}) async-start(bf16[16,4,21504]{2,1,0:T(4,128)(2,1)} %reshape_squeeze.3), calls=%async_computation | async-start | bytes 5505024 | tf_op jit(solution)/shard_map/all_to_all | solution.py:117
  23.9 41.4 %all-to-all-done = bf16[16,4,21504]{2,1,0:T(4,128)(2,1)} async-done(((bf16[16,4,21504]{2,1,0:T(4,128)(2,1)}), bf16[16,4,21504]{2,1,0:T(4,128)(2,1)}, u32[]{:S(2)}, u32[]{:S(2)}) %all-to-all-start) | async-done | bytes 2752544 | tf_op jit(solution)/shard_map/all_to_all | solution.py:117
  65.4 6.1 %gather_fusion.2 = bf16[16,4,21504]{2,1,0:T(4,128)(2,1)} fusion(bf16[16,4,21504]{2,1,0:T(4,128)(2,1)} %all-to-all-done, s32[1024]{0:T(1024)S(1)} %pad_clamp_fusion), kind=kCustom, calls=%fused_computation.2 | custom fusion | bytes 5505088 | tf_op jit(solution)/shard_map/jit(_take)/gather | solution.py:119
  71.5 4.6 %broadcast_select_fusion = bf16[16,4,21504]{2,1,0:T(4,128)(2,1)} fusion(bf16[16,4,21504]{2,1,0:T(4,128)(2,1)} %gather_fusion.2, pred[16]{0:T(512)(128)(4,1)S(1)} %compare_and_fusion.1), kind=kLoop, calls=%fused_computation.19 | loop fusion | flops 1376256 | bytes 5505040 | tf_op jit(solution)/shard_map/jit(_take)/select_n | solution.py:119
  76.1 13.9 %all-to-all-start.1 = ((bf16[16,4,21504]{2,1,0:T(4,128)(2,1)}), bf16[16,4,21504]{2,1,0:T(4,128)(2,1)}, u32[]{:S(2)}, u32[]{:S(2)}) async-start(bf16[16,4,21504]{2,1,0:T(4,128)(2,1)} %broadcast_select_fusion), calls=%async_computation.1 | async-start | bytes 5505024 | tf_op jit(solution)/shard_map/all_to_all | solution.py:120
  97.9 44.7 %all-to-all-done.1 = bf16[16,4,21504]{2,1,0:T(4,128)(2,1)} async-done(((bf16[16,4,21504]{2,1,0:T(4,128)(2,1)}), bf16[16,4,21504]{2,1,0:T(4,128)(2,1)}, u32[]{:S(2)}, u32[]{:S(2)}) %all-to-all-start.1) | async-done | bytes 2752544 | tf_op jit(solution)/shard_map/all_to_all | solution.py:120
  142.5 4.3 %squeeze.61 = bf16[64,21504]{1,0:T(8,128)(2,1)} reshape(bf16[16,4,21504]{2,1,0:T(4,128)(2,1)} %all-to-all-done.1) | data formatting | bytes 5505024 | tf_op jit(solution)/shard_map/squeeze | solution.py:120
  159.3 156.3 %while.22 = (s32[]{:T(128)}, f32[4,512]{1,0:T(4,128)S(1)}, f32[4,512]{1,0:T(4,128)S(1)}, f32[4,512,128]{2,1,0:T(8,128)S(1)}, bf16[2,128,512]{1,2,0:T(8,128)(2,1)...) while((s32[]{:T(128)}, f32[4,512]{1,0:T(4,128)S(1)}, ...), condition=%wide.region_8.9_spmd.clone, body=%wide.region_5.8_spmd.clone.sunk | while | flops 136614176 | bytes 8554928 | solution.py:172
  165.4 10.3 %collective-permute-done = bf16[2,128,512]{1,2,0:T(8,128)(2,1)S(1)} collective-permute-done((bf16[2,128,512]{1,2,0:T(8,128)(2,1)S(1)}, bf16[2,128,512]{1,2,0:T(8,128)(2,1)S(1)}, u32[]{:S(2)}, u32[]{:S(2)}) %collective-permute-start) | collective-permute-done | bytes 262176 | tf_op jit(solution)/shard_map/while/body/eval_jaxpr/ppermute | solution.py:19
  182.5 3.1 collective-permute-done
  192.4 3.1 collective-permute-done
  202.3 3.1 collective-permute-done
  212.2 3.1 collective-permute-done
  222.1 3.1 collective-permute-done
  232.0 3.1 collective-permute-done
  241.9 3.1 collective-permute-done
  251.8 3.1 collective-permute-done
  261.7 3.1 collective-permute-done
  271.6 3.1 collective-permute-done
  281.5 3.1 collective-permute-done
  291.4 3.1 collective-permute-done
  301.3 3.1 collective-permute-done
  316.8 3.3 %fusion.7 = bf16[128,4096]{1,0:T(8,128)(2,1)} fusion(bf16[128,2048]{1,0:T(8,128)(2,1)S(1)} %convert_element_type.87, bf16[64,21504]{1,0:T(8,128)(2,1)} %squeeze.61), kind=kOutput, calls=%fused_computation.18 | convolution fusion | flops 101720064 | bytes 2359296 | tf_op jit(solution)/shard_map/dot_general | solution.py:92
  (313 shorter events, 66.5 us)
Async XLA Ops:
  0.6 146.2 %copy-start = (bf16[128,4096]{1,0:T(8,128)(2,1)S(1)}, bf16[128,4096]{1,0:T(8,128)(2,1)}, u32[]{:S(2)}) copy-start(bf16[128,4096]{1,0:T(8,128)(2,1)} %param.10) | copy-start | bytes 3145732
  5.2 7.6 %copy-start.8 = (s32[3]{0:T(128)S(1)}, s32[3]{0:T(128)}, u32[]{:S(2)}) copy-start(s32[3]{0:T(128)} %param.15) | copy-start | bytes 40
  5.2 15.6 %copy-start.7 = (s32[3]{0:T(128)S(1)}, s32[3]{0:T(128)}, u32[]{:S(2)}) copy-start(s32[3]{0:T(128)} %param.16) | copy-start | bytes 40
  5.2 18.0 %copy-start.1 = (s32[16]{0:T(128)S(1)}, s32[16]{0:T(128)}, u32[]{:S(2)}) copy-start(s32[16]{0:T(128)} %param.17) | copy-start | bytes 196
  5.2 60.2 %all-to-all-start = ((bf16[16,4,21504]{2,1,0:T(4,128)(2,1)}), bf16[16,4,21504]{2,1,0:T(4,128)(2,1)}, u32[]{:S(2)}, u32[]{:S(2)}) async-start(bf16[16,4,21504]{2,1,0:T(4,128)(2,1)} %reshape_squeeze.3), calls=%async_computation | async-start | bytes 5505024 | tf_op jit(solution)/shard_map/all_to_all | solution.py:117
  76.1 66.5 %all-to-all-start.1 = ((bf16[16,4,21504]{2,1,0:T(4,128)(2,1)}), bf16[16,4,21504]{2,1,0:T(4,128)(2,1)}, u32[]{:S(2)}, u32[]{:S(2)}) async-start(bf16[16,4,21504]{2,1,0:T(4,128)(2,1)} %broadcast_select_fusion), calls=%async_computation.1 | async-start | bytes 5505024 | tf_op jit(solution)/shard_map/all_to_all | solution.py:120
  97.9 49.0 %copy-start.4 = (bf16[128,2048]{1,0:T(8,128)(2,1)S(1)}, bf16[128,2048]{1,0:T(8,128)(2,1)}, u32[]{:S(2)}) copy-start(bf16[128,2048]{1,0:T(8,128)(2,1)} %param.11) | copy-start | bytes 1572868
  153.7 1.9 copy-start.6
  159.3 16.5 %collective-permute-start = (bf16[2,128,512]{1,2,0:T(8,128)(2,1)S(1)}, bf16[2,128,512]{1,2,0:T(8,128)(2,1)S(1)}, u32[]{:S(2)}, u32[]{:S(2)}) collective-permute-start(bf16[2,128,512]{1,2,0:T(8,128)(2,1)S(1)} %get-tuple-element.461), channel_id=1, source_target_pairs={{15,0},{0,1},{1,2},{2,3},{3,4},{4,5},{5,6},{6,7},{7,8},{8,9},{9,10... | collective-permute-start | bytes 786440 | tf_op jit(solution)/shard_map/while/body/eval_jaxpr/ppermute | solution.py:19
  177.1 8.5 %collective-permute-start = (bf16[2,128,512]{1,2,0:T(8,128)(2,1)S(1)}, bf16[2,128,512]{1,2,0:T(8,128)(2,1)S(1)}, u32[]{:S(2)}, u32[]{:S(2)}) collective-permute-start(bf16[2,128,512]{1,2,0:T(8,128)(2,1)S(1)} %get-tuple-element.461), channel_id=1, source_target_pairs={{15,0},{0,1},{1,2},{2,3},{3,4},{4,5},{5,6},{6,7},{7,8},{8,9},{9,10... | collective-permute-start | bytes 786440 | tf_op jit(solution)/shard_map/while/body/eval_jaxpr/ppermute | solution.py:19
  187.0 8.5 %collective-permute-start = (bf16[2,128,512]{1,2,0:T(8,128)(2,1)S(1)}, bf16[2,128,512]{1,2,0:T(8,128)(2,1)S(1)}, u32[]{:S(2)}, u32[]{:S(2)}) collective-permute-start(bf16[2,128,512]{1,2,0:T(8,128)(2,1)S(1)} %get-tuple-element.461), channel_id=1, source_target_pairs={{15,0},{0,1},{1,2},{2,3},{3,4},{4,5},{5,6},{6,7},{7,8},{8,9},{9,10... | collective-permute-start | bytes 786440 | tf_op jit(solution)/shard_map/while/body/eval_jaxpr/ppermute | solution.py:19
  196.9 8.5 %collective-permute-start = (bf16[2,128,512]{1,2,0:T(8,128)(2,1)S(1)}, bf16[2,128,512]{1,2,0:T(8,128)(2,1)S(1)}, u32[]{:S(2)}, u32[]{:S(2)}) collective-permute-start(bf16[2,128,512]{1,2,0:T(8,128)(2,1)S(1)} %get-tuple-element.461), channel_id=1, source_target_pairs={{15,0},{0,1},{1,2},{2,3},{3,4},{4,5},{5,6},{6,7},{7,8},{8,9},{9,10... | collective-permute-start | bytes 786440 | tf_op jit(solution)/shard_map/while/body/eval_jaxpr/ppermute | solution.py:19
  206.8 8.5 %collective-permute-start = (bf16[2,128,512]{1,2,0:T(8,128)(2,1)S(1)}, bf16[2,128,512]{1,2,0:T(8,128)(2,1)S(1)}, u32[]{:S(2)}, u32[]{:S(2)}) collective-permute-start(bf16[2,128,512]{1,2,0:T(8,128)(2,1)S(1)} %get-tuple-element.461), channel_id=1, source_target_pairs={{15,0},{0,1},{1,2},{2,3},{3,4},{4,5},{5,6},{6,7},{7,8},{8,9},{9,10... | collective-permute-start | bytes 786440 | tf_op jit(solution)/shard_map/while/body/eval_jaxpr/ppermute | solution.py:19
  216.7 8.5 %collective-permute-start = (bf16[2,128,512]{1,2,0:T(8,128)(2,1)S(1)}, bf16[2,128,512]{1,2,0:T(8,128)(2,1)S(1)}, u32[]{:S(2)}, u32[]{:S(2)}) collective-permute-start(bf16[2,128,512]{1,2,0:T(8,128)(2,1)S(1)} %get-tuple-element.461), channel_id=1, source_target_pairs={{15,0},{0,1},{1,2},{2,3},{3,4},{4,5},{5,6},{6,7},{7,8},{8,9},{9,10... | collective-permute-start | bytes 786440 | tf_op jit(solution)/shard_map/while/body/eval_jaxpr/ppermute | solution.py:19
  226.6 8.5 %collective-permute-start = (bf16[2,128,512]{1,2,0:T(8,128)(2,1)S(1)}, bf16[2,128,512]{1,2,0:T(8,128)(2,1)S(1)}, u32[]{:S(2)}, u32[]{:S(2)}) collective-permute-start(bf16[2,128,512]{1,2,0:T(8,128)(2,1)S(1)} %get-tuple-element.461), channel_id=1, source_target_pairs={{15,0},{0,1},{1,2},{2,3},{3,4},{4,5},{5,6},{6,7},{7,8},{8,9},{9,10... | collective-permute-start | bytes 786440 | tf_op jit(solution)/shard_map/while/body/eval_jaxpr/ppermute | solution.py:19
  236.5 8.5 %collective-permute-start = (bf16[2,128,512]{1,2,0:T(8,128)(2,1)S(1)}, bf16[2,128,512]{1,2,0:T(8,128)(2,1)S(1)}, u32[]{:S(2)}, u32[]{:S(2)}) collective-permute-start(bf16[2,128,512]{1,2,0:T(8,128)(2,1)S(1)} %get-tuple-element.461), channel_id=1, source_target_pairs={{15,0},{0,1},{1,2},{2,3},{3,4},{4,5},{5,6},{6,7},{7,8},{8,9},{9,10... | collective-permute-start | bytes 786440 | tf_op jit(solution)/shard_map/while/body/eval_jaxpr/ppermute | solution.py:19
  246.4 8.5 %collective-permute-start = (bf16[2,128,512]{1,2,0:T(8,128)(2,1)S(1)}, bf16[2,128,512]{1,2,0:T(8,128)(2,1)S(1)}, u32[]{:S(2)}, u32[]{:S(2)}) collective-permute-start(bf16[2,128,512]{1,2,0:T(8,128)(2,1)S(1)} %get-tuple-element.461), channel_id=1, source_target_pairs={{15,0},{0,1},{1,2},{2,3},{3,4},{4,5},{5,6},{6,7},{7,8},{8,9},{9,10... | collective-permute-start | bytes 786440 | tf_op jit(solution)/shard_map/while/body/eval_jaxpr/ppermute | solution.py:19
  256.3 8.5 %collective-permute-start = (bf16[2,128,512]{1,2,0:T(8,128)(2,1)S(1)}, bf16[2,128,512]{1,2,0:T(8,128)(2,1)S(1)}, u32[]{:S(2)}, u32[]{:S(2)}) collective-permute-start(bf16[2,128,512]{1,2,0:T(8,128)(2,1)S(1)} %get-tuple-element.461), channel_id=1, source_target_pairs={{15,0},{0,1},{1,2},{2,3},{3,4},{4,5},{5,6},{6,7},{7,8},{8,9},{9,10... | collective-permute-start | bytes 786440 | tf_op jit(solution)/shard_map/while/body/eval_jaxpr/ppermute | solution.py:19
  266.2 8.5 %collective-permute-start = (bf16[2,128,512]{1,2,0:T(8,128)(2,1)S(1)}, bf16[2,128,512]{1,2,0:T(8,128)(2,1)S(1)}, u32[]{:S(2)}, u32[]{:S(2)}) collective-permute-start(bf16[2,128,512]{1,2,0:T(8,128)(2,1)S(1)} %get-tuple-element.461), channel_id=1, source_target_pairs={{15,0},{0,1},{1,2},{2,3},{3,4},{4,5},{5,6},{6,7},{7,8},{8,9},{9,10... | collective-permute-start | bytes 786440 | tf_op jit(solution)/shard_map/while/body/eval_jaxpr/ppermute | solution.py:19
  276.1 8.5 %collective-permute-start = (bf16[2,128,512]{1,2,0:T(8,128)(2,1)S(1)}, bf16[2,128,512]{1,2,0:T(8,128)(2,1)S(1)}, u32[]{:S(2)}, u32[]{:S(2)}) collective-permute-start(bf16[2,128,512]{1,2,0:T(8,128)(2,1)S(1)} %get-tuple-element.461), channel_id=1, source_target_pairs={{15,0},{0,1},{1,2},{2,3},{3,4},{4,5},{5,6},{6,7},{7,8},{8,9},{9,10... | collective-permute-start | bytes 786440 | tf_op jit(solution)/shard_map/while/body/eval_jaxpr/ppermute | solution.py:19
  286.0 8.5 %collective-permute-start = (bf16[2,128,512]{1,2,0:T(8,128)(2,1)S(1)}, bf16[2,128,512]{1,2,0:T(8,128)(2,1)S(1)}, u32[]{:S(2)}, u32[]{:S(2)}) collective-permute-start(bf16[2,128,512]{1,2,0:T(8,128)(2,1)S(1)} %get-tuple-element.461), channel_id=1, source_target_pairs={{15,0},{0,1},{1,2},{2,3},{3,4},{4,5},{5,6},{6,7},{7,8},{8,9},{9,10... | collective-permute-start | bytes 786440 | tf_op jit(solution)/shard_map/while/body/eval_jaxpr/ppermute | solution.py:19
  295.8 8.5 %collective-permute-start = (bf16[2,128,512]{1,2,0:T(8,128)(2,1)S(1)}, bf16[2,128,512]{1,2,0:T(8,128)(2,1)S(1)}, u32[]{:S(2)}, u32[]{:S(2)}) collective-permute-start(bf16[2,128,512]{1,2,0:T(8,128)(2,1)S(1)} %get-tuple-element.461), channel_id=1, source_target_pairs={{15,0},{0,1},{1,2},{2,3},{3,4},{4,5},{5,6},{6,7},{7,8},{8,9},{9,10... | collective-permute-start | bytes 786440 | tf_op jit(solution)/shard_map/while/body/eval_jaxpr/ppermute | solution.py:19
  305.7 8.5 %collective-permute-start = (bf16[2,128,512]{1,2,0:T(8,128)(2,1)S(1)}, bf16[2,128,512]{1,2,0:T(8,128)(2,1)S(1)}, u32[]{:S(2)}, u32[]{:S(2)}) collective-permute-start(bf16[2,128,512]{1,2,0:T(8,128)(2,1)S(1)} %get-tuple-element.461), channel_id=1, source_target_pairs={{15,0},{0,1},{1,2},{2,3},{3,4},{4,5},{5,6},{6,7},{7,8},{8,9},{9,10... | collective-permute-start | bytes 786440 | tf_op jit(solution)/shard_map/while/body/eval_jaxpr/ppermute | solution.py:19
  316.8 3.3 %copy-start.3 = (bf16[128,2048]{1,0:T(8,128)(2,1)}, bf16[128,2048]{1,0:T(8,128)(2,1)S(1)}, u32[]{:S(2)}) copy-start(bf16[128,2048]{1,0:T(8,128)(2,1)S(1)} %convert_element_type.87) | copy-start | bytes 1572868
  (2 other events, 2.5 us)
where the time goes:
time: 322 us; the launch traced here: 320 us
  waiting for transfers between devices  140 us (43%)
  loops' own time  60.7 us (19%)
  local copies, waits for them, and re-layouts  42.6 us (13%)
  matrix products  27 us (8%)
  starting transfers between devices  23.1 us (7%)
  other arithmetic  15.1 us (5%)
  between operations  11.5 us (4%)
    another operation x1, loops' own time, body(): lax.fori_loop(1, shards, advance, (running, paired_key_value))  60.7 us
    ppermute x15, waiting for transfers between devices, shifted(): return lax.ppermute(block, axis, route)  54.1 us
    all_to_all x1, waiting for transfers between devices, body(): lax.all_to_all(outgoing, 'ctx', split_axis=0, concat_axis=1, tiled=True)[0]  44.7 us
    all_to_all x1, waiting for transfers between devices, body(): lax.all_to_all(pieces, 'ctx', split_axis=0, concat_axis=0, tiled=True)  41.4 us
    all_to_all x1, starting transfers between devices, body(): lax.all_to_all(outgoing, 'ctx', split_axis=0, concat_axis=1, tiled=True)[0]  13.9 us
    dot_general x16, matrix products, attend(): jnp.einsum('vel,lvw->vew', attention_weight.astype(jnp.bfloat16), value_b...  11.8 us
    dynamic_slice x16, local copies, waits for them, and re-layouts, attend(): same_request = request_of[source_packed] == own_request  9.45 us
    dynamic_slice x16, local copies, waits for them, and re-layouts, attend(): source_packed = packed_of[source]  9.39 us
  transfers between devices with their start and end apart: 17, of which 17 were waited for; matrix products, arithmetic and copies ran while one was open for 9% of the time, Pallas kernels for 0%

commit v1 on v0

v1 whole, which is shorter than its diff:
```python
import functools

import jax
import jax.numpy as jnp
from jax import lax
from jax.experimental import pallas as pl
from jax.experimental.pallas import tpu as pltpu
from jax.sharding import PartitionSpec as P

HEAD_SIZE = 128
QUERY_HEADS = 16
KEY_VALUE_HEADS = 4
GROUP_SPLIT = QUERY_HEADS // KEY_VALUE_HEADS

adapter_scale = 0.5
rope_theta = 500000.0
score_masked = -1e30

ROW_BLOCKS = 4
CHUNKS = 8
VMEM_LIMIT = 48 * 1024 * 1024


def request_layout(request_shards, shards):
    starts = jnp.cumsum(request_shards) - request_shards
    shard_ids = jnp.arange(shards, dtype=jnp.int32)
    request_of = jnp.sum((starts[None, :] <= shard_ids[:, None]).astype(jnp.int32), axis=1) - 1
    longest = jnp.argmax(request_shards)
    offset = (starts[longest] + request_shards[longest] // 2) % shards
    packed_of = (shard_ids + offset) % shards
    return (request_of, starts, packed_of)


def rope_tables(positions):
    half_dim = HEAD_SIZE // 2
    frequency = rope_theta ** (-(jnp.arange(half_dim, dtype=jnp.float32) * 2.0) / HEAD_SIZE)
    angles = positions.astype(jnp.float32)[:, None] * frequency[None, :]
    cosines = jnp.cos(angles)
    sines = jnp.sin(angles)
    return (jnp.concatenate([cosines, cosines], 1), jnp.concatenate([-sines, sines], 1))


class Parts:
    def __init__(self, model_width, query_width, key_width):
        d, q, k = model_width, query_width, key_width
        up = 3 * d
        self.kv = ((d, d // CHUNKS), (2 * d, d // CHUNKS), (up + q, 2 * k // CHUNKS))
        self.q = ((0, d // CHUNKS), (up, q // CHUNKS))
        self.o = ((up + q + 2 * k, q // CHUNKS), (up + 2 * q + 2 * k, d // CHUNKS))
        self.all = (self.kv, self.q, self.o)
        self.widths = tuple(sum(w for _, w in part) for part in self.all)


def pack_kernel(parts, halves, x_ref, bank_ref, *outs):
    own_half = x_ref[0]
    for block in range(outs[0].shape[0]):
        piece = block % (ROW_BLOCKS * CHUNKS // halves)
        rows = pl.ds((piece % ROW_BLOCKS) * 16, 16)
        chunk = (piece // ROW_BLOCKS) * halves + own_half
        for part, out in zip(parts.all, outs):
            at = 0
            for first, width in part:
                start = pl.multiple_of(first + chunk * width, 128)
                out[block, :, at : at + width] = bank_ref[0, rows, pl.ds(start, width)]
                at += width


def pack(parts, halves, shards, own_half, bank):
    return pl.pallas_call(
        functools.partial(pack_kernel, parts, halves),
        out_shape=[jax.ShapeDtypeStruct((shards, 16, w), bank.dtype) for w in parts.widths],
        in_specs=[
            pl.BlockSpec(memory_space=pltpu.SMEM),
            pl.BlockSpec(memory_space=pltpu.VMEM),
        ],
        out_specs=[pl.BlockSpec(memory_space=pltpu.VMEM)] * 3,
        compiler_params=pltpu.CompilerParams(vmem_limit_bytes=VMEM_LIMIT),
        name="pack",
    )(own_half.reshape(1), bank)


def pick_kernel(count, ids_ref, spread_ref, *outs_and_sem):
    outs, sem = outs_and_sem[:-1], outs_and_sem[-1]
    copies = []
    for out_index, out in enumerate(outs):
        for slot in range(count):
            copies.append(
                pltpu.make_async_copy(
                    spread_ref.at[ids_ref[out_index * count + slot]],
                    out.at[slot],
                    sem.at[len(copies)],
                )
            )
    for copy in copies:
        copy.start()
    for copy in copies:
        copy.wait()


def pick(ids, spread, count):
    outputs = ids.shape[0] // count
    shape = jax.ShapeDtypeStruct((count,) + spread.shape[1:], spread.dtype)
    return pl.pallas_call(
        functools.partial(pick_kernel, count),
        out_shape=[shape] * outputs,
        in_specs=[
            pl.BlockSpec(memory_space=pltpu.SMEM),
            pl.BlockSpec(memory_space=pl.ANY),
        ],
        out_specs=[pl.BlockSpec(memory_space=pl.ANY)] * outputs,
        scratch_shapes=[pltpu.SemaphoreType.DMA((count * outputs,))],
        name="pick",
    )(ids, spread)


def chunk_of(place, half, halves, own_half):
    if halves == 1:
        return place
    return place * halves + (own_half if half == 0 else 1 - own_half)


def factor(piece_ref, place, half, at, width):
    rows = piece_ref[place * ROW_BLOCKS : (place + 1) * ROW_BLOCKS, half, :, at : at + width]
    return rows.reshape(ROW_BLOCKS * 16, width)


def at_chunk(ref, chunk, width):
    return ref[:, pl.ds(pl.multiple_of(chunk * width, 128), width)]


def dot_nt(a, b):
    return lax.dot_general(a, b, (((1,), (1,)), ((), ())), preferred_element_type=jnp.float32)


def turn(x, cosines, sines):
    return x * cosines + pltpu.roll(x, HEAD_SIZE // 2, 1) * sines


def kv_kernel(halves, s_ref, hidden_ref, key_ref, value_ref, cos_ref, sin_ref, piece_ref, out_ref):
    own_half = s_ref[1]
    places = [(p, h) for p in range(CHUNKS // halves) for h in range(halves)]
    d = hidden_ref.shape[1] // CHUNKS
    low = jnp.zeros((hidden_ref.shape[0], 2 * ROW_BLOCKS * 16), jnp.float32)
    for p, h in places:
        chunk = chunk_of(p, h, halves, own_half)
        down = jnp.concatenate(
            [factor(piece_ref, p, h, 0, d), factor(piece_ref, p, h, d, d)], axis=0
        )
        low += dot_nt(at_chunk(hidden_ref, chunk, d), down)
    low = low.astype(jnp.bfloat16)
    low_key, low_value = low[:, : ROW_BLOCKS * 16], low[:, ROW_BLOCKS * 16 :]
    width = 2 * key_ref.shape[1] // CHUNKS
    cosines, sines = cos_ref[...], sin_ref[...]
    for p, h in places:
        chunk = chunk_of(p, h, halves, own_half)
        up = factor(piece_ref, p, h, 2 * d, width)
        is_key = p < CHUNKS // halves // 2
        update = jnp.dot(low_key if is_key else low_value, up, preferred_element_type=jnp.float32)
        place = chunk if is_key else chunk - CHUNKS // 2
        frozen = at_chunk(key_ref if is_key else value_ref, place, width)
        result = frozen.astype(jnp.float32) + adapter_scale * update
        if is_key:
            result = turn(result, cosines, sines)
        start = pl.multiple_of(chunk * width, 128)
        out_ref[:, pl.ds(start, width)] = result.astype(jnp.bfloat16)


def query_kernel(halves, s_ref, hidden_ref, query_ref, cos_ref, sin_ref, piece_ref, out_ref):
    own_half = s_ref[1]
    places = [(p, h) for p in range(CHUNKS // halves) for h in range(halves)]
    d = hidden_ref.shape[1] // CHUNKS
    low = jnp.zeros((hidden_ref.shape[0], ROW_BLOCKS * 16), jnp.float32)
    for p, h in places:
        chunk = chunk_of(p, h, halves, own_half)
        low += dot_nt(at_chunk(hidden_ref, chunk, d), factor(piece_ref, p, h, 0, d))
    low = low.astype(jnp.bfloat16)
    width = query_ref.shape[1] // CHUNKS
    cosines, sines = cos_ref[...], sin_ref[...]
    for p, h in places:
        chunk = chunk_of(p, h, halves, own_half)
        up = factor(piece_ref, p, h, d, width)
        update = jnp.dot(low, up, preferred_element_type=jnp.float32)
        result = at_chunk(query_ref, chunk, width).astype(jnp.float32) + adapter_scale * update
        for head in range(width // HEAD_SIZE):
            turned = turn(result[:, head * HEAD_SIZE : (head + 1) * HEAD_SIZE], cosines, sines)
            start = pl.multiple_of(chunk * width + head * HEAD_SIZE, 128)
            out_ref[:, pl.ds(start, HEAD_SIZE)] = turned.astype(jnp.bfloat16)


def piece_spec(halves, requests, width):
    return pl.BlockSpec(
        (ROW_BLOCKS * CHUNKS // halves, halves, None, 16, width),
        lambda i, s: (0, 0, s[0], 0, 0),
    )


def whole_spec(shape):
    return pl.BlockSpec(shape, lambda i, s: (0,) * len(shape))


def project(kernel, halves, scalars, arrays, pieces, out_shape, flops, name):
    return pl.pallas_call(
        functools.partial(kernel, halves),
        out_shape=out_shape,
        grid_spec=pltpu.PrefetchScalarGridSpec(
            num_scalar_prefetch=1,
            grid=(1,),
            in_specs=[whole_spec(a.shape) for a in arrays]
            + [piece_spec(halves, pieces.shape[2], pieces.shape[4])],
            out_specs=whole_spec(out_shape.shape),
        ),
        compiler_params=pltpu.CompilerParams(vmem_limit_bytes=VMEM_LIMIT),
        cost_estimate=pl.CostEstimate(flops=flops, bytes_accessed=4 << 20, transcendentals=0),
        name=name,
    )(scalars, *arrays, pieces)


def attend_kernel(
    halves, shards, s_ref, query_ref, piece_ref, kv_ref, out_ref, extra_ref,
    block, best, total, acc, low_ref, sem,
):
    own_half, own_index, count = s_ref[1], s_ref[2], s_ref[3]
    tokens = query_ref.shape[0]
    rows = GROUP_SPLIT * tokens
    key_width = KEY_VALUE_HEADS * HEAD_SIZE
    factor_base2 = 1.4426950408889634 / (HEAD_SIZE**0.5)

    def fetch(step):
        source = lax.rem(own_index - step + shards, shards)
        return pltpu.make_async_copy(
            kv_ref.at[source],
            block.at[pl.ds(pl.multiple_of(step * tokens, tokens), tokens)],
            sem.at[step],
        )

    lax.fori_loop(0, count, lambda step, c: (fetch(step).start(), c)[1], 0)

    def queries(g):
        heads = [
            query_ref[:, (g * GROUP_SPLIT + j) * HEAD_SIZE : (g * GROUP_SPLIT + j + 1) * HEAD_SIZE]
            for j in range(GROUP_SPLIT)
        ]
        return jnp.concatenate(heads, axis=0)

    def keys_values(first, blocks, g):
        at = pl.ds(pl.multiple_of(first * tokens, tokens), blocks * tokens)
        k = block[at, g * HEAD_SIZE : (g + 1) * HEAD_SIZE]
        v = block[at, key_width + g * HEAD_SIZE : key_width + (g + 1) * HEAD_SIZE]
        return k, v

    fetch(0).wait()
    row = lax.broadcasted_iota(jnp.int32, (rows, tokens), 0) % tokens
    column = lax.broadcasted_iota(jnp.int32, (rows, tokens), 1)
    allowed = column <= row
    for g in range(KEY_VALUE_HEADS):
        k, v = keys_values(0, 1, g)
        score = jnp.where(allowed, dot_nt(queries(g), k) * factor_base2, score_masked)
        high = jnp.max(score, axis=1, keepdims=True)
        weight = jnp.exp2(score - high)
        best[g] = high
        total[g] = jnp.sum(weight, axis=1, keepdims=True)
        acc[g] = jnp.dot(weight.astype(jnp.bfloat16), v, preferred_element_type=jnp.float32)

    def more(first, blocks):
        for step in range(blocks):
            fetch(first + step).wait()
        for g in range(KEY_VALUE_HEADS):
            k, v = keys_values(first, blocks, g)
            score = dot_nt(queries(g), k) * factor_base2
            old = best[g]
            high = jnp.maximum(old, jnp.max(score, axis=1, keepdims=True))
            shrink = jnp.exp2(old - high)
            weight = jnp.exp2(score - high)
            best[g] = high
            total[g] = total[g] * shrink + jnp.sum(weight, axis=1, keepdims=True)
            acc[g] = acc[g] * shrink + jnp.dot(
                weight.astype(jnp.bfloat16), v, preferred_element_type=jnp.float32
            )

    pairs = (count - 1) // 2

    def pair(i, c):
        more(1 + 2 * i, 2)
        return c

    lax.fori_loop(0, pairs, pair, 0)

    @pl.when(count - 1 > 2 * pairs)
    def _():
        more(count - 1, 1)

    for g in range(KEY_VALUE_HEADS):
        result = (acc[g] / total[g]).astype(jnp.bfloat16)
        for j in range(GROUP_SPLIT):
            at = (g * GROUP_SPLIT + j) * HEAD_SIZE
            out_ref[:, at : at + HEAD_SIZE] = result[j * tokens : (j + 1) * tokens]

    q_width = query_ref.shape[1] // CHUNKS
    d = extra_ref.shape[1] // CHUNKS
    places = [(p, h) for p in range(CHUNKS // halves) for h in range(halves)]
    low = jnp.zeros((tokens, ROW_BLOCKS * 16), jnp.float32)
    for p, h in places:
        chunk = chunk_of(p, h, halves, own_half)
        low += dot_nt(at_chunk(out_ref, chunk, q_width), factor(piece_ref, p, h, 0, q_width))
    low = low.astype(jnp.bfloat16)
    for p, h in places:
        chunk = chunk_of(p, h, halves, own_half)
        up = factor(piece_ref, p, h, q_width, d)
        start = pl.multiple_of(chunk * d, 128)
        result = adapter_scale * jnp.dot(low, up, preferred_element_type=jnp.float32)
        extra_ref[:, pl.ds(start, d)] = result.astype(jnp.bfloat16)


def attend(halves, shards, scalars, query, pieces, kv, model_width):
    tokens, query_width = query.shape
    reach = shards // 2 + 1
    rows = GROUP_SPLIT * tokens
    out_shape = [
        jax.ShapeDtypeStruct((tokens, query_width), jnp.bfloat16),
        jax.ShapeDtypeStruct((tokens, model_width), jnp.bfloat16),
    ]
    return pl.pallas_call(
        functools.partial(attend_kernel, halves, shards),
        out_shape=out_shape,
        grid_spec=pltpu.PrefetchScalarGridSpec(
            num_scalar_prefetch=1,
            grid=(1,),
            in_specs=[
                whole_spec(query.shape),
                piece_spec(halves, pieces.shape[2], pieces.shape[4]),
                pl.BlockSpec(memory_space=pl.ANY),
            ],
            out_specs=[whole_spec(o.shape) for o in out_shape],
            scratch_shapes=[
                pltpu.VMEM((reach * tokens, kv.shape[2]), jnp.bfloat16),
                pltpu.VMEM((KEY_VALUE_HEADS, rows, 1), jnp.float32),
                pltpu.VMEM((KEY_VALUE_HEADS, rows, 1), jnp.float32),
                pltpu.VMEM((KEY_VALUE_HEADS, rows, HEAD_SIZE), jnp.float32),
                pltpu.VMEM((tokens, ROW_BLOCKS * 16), jnp.float32),
                pltpu.SemaphoreType.DMA((reach,)),
            ],
        ),
        compiler_params=pltpu.CompilerParams(vmem_limit_bytes=VMEM_LIMIT),
        cost_estimate=pl.CostEstimate(
            flops=2_000_000_000, bytes_accessed=8 << 20, transcendentals=4 << 20
        ),
        name="attend",
    )(scalars, query, pieces, kv)


def body(
    hidden,
    frozen_query,
    frozen_key,
    frozen_value,
    adapter_bank,
    request_shards,
    request_adapter,
    adapter_owner,
):
    shards = lax.axis_size("ctx")
    groups = lax.axis_size("groups")
    own_index = lax.axis_index("ctx").astype(jnp.int32)
    tokens, model_width = hidden.shape
    requests = request_shards.shape[0]
    halves = 2 if groups == 2 and 2 * shards == ROW_BLOCKS * CHUNKS else 1
    own_half = lax.axis_index("groups").astype(jnp.int32) if halves == 2 else jnp.int32(0)
    parts = Parts(model_width, frozen_query.shape[1], frozen_key.shape[1])

    packed = pack(parts, halves, shards, own_half, adapter_bank)
    spread = [lax.all_to_all(p, "ctx", split_axis=0, concat_axis=0, tiled=True) for p in packed]

    request_of, starts, packed_of = request_layout(request_shards, shards)
    own_packed = packed_of[own_index]
    own_request = request_of[own_packed]
    first = starts[own_request]
    positions = (own_packed - first) * tokens + jnp.arange(tokens, dtype=jnp.int32)
    cosines, sines = rope_tables(positions)
    scalars = jnp.stack(
        [own_request, own_half, own_index, own_packed - first + 1]
    ).astype(jnp.int32)

    wanted = request_adapter
    if halves == 2:
        theirs = lax.ppermute(request_adapter, "groups", [(0, 1), (1, 0)])
        wanted = jnp.concatenate([request_adapter, theirs])
    ids = adapter_owner[wanted].astype(jnp.int32)

    gathered = []
    for s in spread:
        picked = pick(ids, s, requests)
        if halves == 2:
            arrived = lax.ppermute(picked[1], "groups", [(0, 1), (1, 0)])
            piece = jnp.stack([picked[0], arrived])
        else:
            piece = picked[0][None]
        gathered.append(lax.all_gather(piece, "ctx"))

    bf16 = jnp.bfloat16
    kv = project(
        kv_kernel, halves, scalars, (hidden, frozen_key, frozen_value, cosines, sines),
        gathered[0], jax.ShapeDtypeStruct((tokens, 2 * frozen_key.shape[1]), bf16),
        150_000_000, "keys_values",
    )
    all_kv = lax.all_gather(kv, "ctx")
    query = project(
        query_kernel, halves, scalars, (hidden, frozen_query, cosines, sines),
        gathered[1], jax.ShapeDtypeStruct(frozen_query.shape, bf16),
        100_000_000, "queries",
    )
    return tuple(attend(halves, shards, scalars, query, gathered[2], all_kv, model_width))


def solution(mesh):
    return jax.shard_map(
        body,
        mesh=mesh,
        in_specs=(
            P(("groups", "ctx"), None),
            P(("groups", "ctx"), None),
            P(("groups", "ctx"), None),
            P(("groups", "ctx"), None),
            P("ctx", None, None),
            P("groups"),
            P("groups"),
            P(),
        ),
        out_specs=(P(("groups", "ctx"), None), P(("groups", "ctx"), None)),
        check_vma=False,
    )
```

time: 322 us -> 269 us (0.84); the launches traced: 320 us -> 264 us
  loops' own time: 60.7 us -> 0 us
  blocking collectives: 0 us -> 43.2 us
  Pallas kernels: 0 us -> 36 us
  local copies, waits for them, and re-layouts: 42.6 us -> 12.2 us
  matrix products: 27 us -> 0 us
  between operations: 11.5 us -> 23.6 us
  waiting for transfers between devices: 140 us -> 128 us
  starting transfers between devices: 23.1 us -> 13.8 us
  other arithmetic: 15.1 us -> 6.85 us
    all_gather x0 -> x4, waiting for transfers between devices: none -> 106 us  [the longest x3 53.7 us: body(): gathered.append(lax.all_gather(piece, 'ctx'))]
    all_to_all x2 -> x1, waiting for transfers between devices: 86.1 us -> 10.6 us  [body(): lax.all_to_all(p, 'ctx', split_axis=0, concat_axis=0, tiled=True)]
    another operation x1 -> x0, loops' own time: 60.7 us -> none  [body(): lax.fori_loop(1, shards, advance, (running, paired_key_value))]
    all_to_all x0 -> x2, blocking collectives: none -> 43.2 us  [body(): lax.all_to_all(p, 'ctx', split_axis=0, concat_axis=0, tiled=True)]
    ppermute x15 -> x4, waiting for transfers between devices: 54.1 us -> 11.8 us  [the longest x3 9.8 us: body(): arrived = lax.ppermute(picked[1], 'groups', [(0, 1), (1, 0)])]
    pallas_call x0 -> x7, Pallas kernels: none -> 36 us  [the longest x3 21.1 us: pick(): pl.pallas_call(functools.partial(pick_kernel, count), out_shape=[shape] *...]
    dot_general x36 -> x0, matrix products: 27 us -> none  [the longest x16 11.8 us: attend(): jnp.einsum('vel,lvw->vew', attention_weight.astype(jnp.bfloat16), value_b...]
    dynamic_slice x33 -> x3, local copies, waits for them, and re-layouts: 19.5 us -> 1.88 us  [the longest x1 0.67 us: body(): own_packed = packed_of[own_index]]
  transfers between devices with their start and end apart: 17 -> 9, of which waited for: 17 -> 8; matrix products, arithmetic and copies ran while one was open for 9% -> 4% of each run, Pallas kernels for 0% -> 6%
where the time goes in v1:
time: 269 us; the launch traced here: 264 us
  waiting for transfers between devices  128 us (48%)
  blocking collectives  43.2 us (16%)
  Pallas kernels  36 us (13%)
  between operations  23.6 us (9%)
  starting transfers between devices  13.8 us (5%)
  local copies, waits for them, and re-layouts  12.2 us (5%)
  other arithmetic  6.85 us (3%)
    all_gather x3, waiting for transfers between devices, body(): gathered.append(lax.all_gather(piece, 'ctx'))  53.7 us
    all_gather x1, waiting for transfers between devices, body(): all_kv = lax.all_gather(kv, 'ctx')  52 us
    all_to_all x2, blocking collectives, body(): lax.all_to_all(p, 'ctx', split_axis=0, concat_axis=0, tiled=True)  43.2 us
    pallas_call x3, Pallas kernels, pick(): pl.pallas_call(functools.partial(pick_kernel, count), out_shape=[shape] *...  21.1 us
    all_to_all x1, waiting for transfers between devices, body(): lax.all_to_all(p, 'ctx', split_axis=0, concat_axis=0, tiled=True)  10.6 us
    pallas_call x1, Pallas kernels, attend(): pl.pallas_call(functools.partial(attend_kernel, halves, shards), out_shap...  10.3 us
    ppermute x3, waiting for transfers between devices, body(): arrived = lax.ppermute(picked[1], 'groups', [(0, 1), (1, 0)])  9.8 us
    unnamed x24, local copies, waits for them, and re-layouts  8.04 us
  transfers between devices with their start and end apart: 9, of which 8 were waited for; matrix products, arithmetic and copies ran while one was open for 4% of the time, Pallas kernels for 6%

profile of v1, /device:TPU:0, one launch (start us, length us, event | category | flops | bytes accessed | tf_op | source)
XLA Modules:
  0.0 263.8 jit_solution(11419241768751725704)
XLA Ops:
  7.2 1.8 copy-done.3
  9.9 7.4 %all-to-all-start.2 = ((bf16[16,16,1152]{2,1,0:T(8,128)(2,1)}), bf16[16,16,1152]{2,1,0:T(8,128)(2,1)S(1)}, u32[]{:S(2)}, u32[]{:S(2)}) async-start(bf16[16,16,1152]{2,1,0:T(8,128)(2,1)} %get-tuple-element.19), calls=%async_computation.2 | async-start | bytes 1179648 | tf_op jit(solution)/shard_map/all_to_all | solution.py:371
  18.9 2.0 collective-permute-done
  22.2 10.6 %all-to-all-done.2.spread_ref = bf16[16,16,1152]{2,1,0:T(8,128)(2,1)S(1)} async-done(((bf16[16,16,1152]{2,1,0:T(8,128)(2,1)}), bf16[16,16,1152]{2,1,0:T(8,128)(2,1)S(1)}, u32[]{:S(2)}, u32[]{:S(2)}) %all-to-all-start.2) | async-done | bytes 589856 | tf_op jit(solution)/shard_map/all_to_all | solution.py:371
  33.7 8.5 %pick.5 = (bf16[3,16,1152]{2,1,0:T(8,128)(2,1)}, bf16[3,16,1152]{2,1,0:T(8,128)(2,1)}) custom-call(s32[6]{0:T(128)} %gather_fusion, bf16[16,16,1152]{2,1,0:T(8,128)(2,1)} %copy-done.9), custom_call_target="tpu_custom_call" | custom-call | tf_op jit(solution)/shard_map/pick/pallas_call | solution.py:103
  43.8 3.7 %collective-permute-done.3 = bf16[3,16,1152]{2,1,0:T(8,128)(2,1)S(1)} collective-permute-done((bf16[3,16,1152]{2,1,0:T(8,128)(2,1)}, bf16[3,16,1152]{2,1,0:T(8,128)(2,1)S(1)}, u32[]{:S(2)}, u32[]{:S(2)}) %collective-permute-start.3) | collective-permute-done | bytes 110624 | tf_op jit(solution)/shard_map/ppermute | solution.py:393
  47.5 1.6 pad_maximum_fusion
  49.1 20.2 %all_to_all.15.spread_ref = bf16[16,16,768]{2,1,0:T(8,128)(2,1)} all-to-all(bf16[16,16,768]{2,1,0:T(8,128)(2,1)S(1)} %get-tuple-element.13), channel_id=1, replica_groups=mesh['groups'=2,'ctx'=16] {'ctx'}, dimensions={0} | all-to-all | bytes 786432 | tf_op jit(solution)/shard_map/all_to_all | solution.py:371
  69.3 6.3 %pick.3 = (bf16[3,16,768]{2,1,0:T(8,128)(2,1)}, bf16[3,16,768]{2,1,0:T(8,128)(2,1)}) custom-call(s32[6]{0:T(128)} %gather_fusion, bf16[16,16,768]{2,1,0:T(8,128)(2,1)} %all_to_all.15.spread_ref), custom_call_target="tpu_custom_call" | custom-call | tf_op jit(solution)/shard_map/pick/pallas_call | solution.py:103
  75.6 1.6 collective-permute-start.1
  77.2 3.0 %collective-permute-done.1 = bf16[3,16,768]{2,1,0:T(8,128)(2,1)S(1)} collective-permute-done((bf16[3,16,768]{2,1,0:T(8,128)(2,1)}, bf16[3,16,768]{2,1,0:T(8,128)(2,1)S(1)}, u32[]{:S(2)}, u32[]{:S(2)}) %collective-permute-start.1) | collective-permute-done | bytes 73760 | tf_op jit(solution)/shard_map/ppermute | solution.py:393
  81.9 23.0 %all_to_all.16.spread_ref = bf16[16,16,768]{2,1,0:T(8,128)(2,1)} all-to-all(bf16[16,16,768]{2,1,0:T(8,128)(2,1)S(1)} %get-tuple-element.16), channel_id=1, replica_groups=mesh['groups'=2,'ctx'=16] {'ctx'}, dimensions={0} | all-to-all | bytes 786432 | tf_op jit(solution)/shard_map/all_to_all | solution.py:371
  104.9 6.3 %pick.4 = (bf16[3,16,768]{2,1,0:T(8,128)(2,1)}, bf16[3,16,768]{2,1,0:T(8,128)(2,1)}) custom-call(s32[6]{0:T(128)} %gather_fusion, bf16[16,16,768]{2,1,0:T(8,128)(2,1)} %all_to_all.16.spread_ref), custom_call_target="tpu_custom_call" | custom-call | tf_op jit(solution)/shard_map/pick/pallas_call | solution.py:103
  111.2 1.6 collective-permute-start.2
  112.8 3.1 %collective-permute-done.2 = bf16[3,16,768]{2,1,0:T(8,128)(2,1)S(1)} collective-permute-done((bf16[3,16,768]{2,1,0:T(8,128)(2,1)}, bf16[3,16,768]{2,1,0:T(8,128)(2,1)S(1)}, u32[]{:S(2)}, u32[]{:S(2)}) %collective-permute-start.2) | collective-permute-done | bytes 73760 | tf_op jit(solution)/shard_map/ppermute | solution.py:393
  115.8 1.6 pad_maximum_fusion.2
  132.2 2.1 copy-done.2
  134.3 2.0 keys_values.1
  136.4 13.6 %all-gather.9.cloned.1.call-done = bf16[32,3,16,768]{3,2,1,0:T(8,128)(2,1)} async-done(((bf16[2,3,16,768]{3,2,1,0:T(8,128)(2,1)}), bf16[32,3,16,768]{3,2,1,0:T(8,128)(2,1)}) %all-gather.9.cloned.1.call-update) | async-done | bytes 2359312 | tf_op jit(solution)/shard_map/all_gather | solution.py:397
  150.0 1.7 copy-done.4
  153.2 40.1 %all-gather.11.cloned.1.call-done = bf16[32,3,16,768]{3,2,1,0:T(8,128)(2,1)} async-done(((bf16[2,3,16,768]{3,2,1,0:T(8,128)(2,1)}), bf16[32,3,16,768]{3,2,1,0:T(8,128)(2,1)}) %all-gather.11.cloned.1.call-update) | async-done | bytes 2359312 | tf_op jit(solution)/shard_map/all_gather | solution.py:397
  193.3 52.0 %all-gather.15.cloned.1.call-done = bf16[2048,1024]{1,0:T(8,128)(2,1)} async-done(((bf16[128,1024]{1,0:T(8,128)(2,1)}), bf16[2048,1024]{1,0:T(8,128)(2,1)}) %all-gather.15.cloned.1.call-update) | async-done | bytes 4194320 | tf_op jit(solution)/shard_map/all_gather | solution.py:405
  245.2 1.7 copy-done.8
  246.9 10.3 %attend.1 = (bf16[128,2048]{1,0:T(8,128)(2,1)}, bf16[128,4096]{1,0:T(8,128)(2,1)}) custom-call(s32[4]{0:T(128)S(1)} %pad_add_fusion.s_ref, bf16[128,2048]{1,0:T(8,128)(2,1)S(1)} %queries.1.query_ref, bf16[16,2,3,16,768]{4,3,2,1,0:T(8,128)(2,1)S(1)} %bitcast.27, bf16[16,128,1024]{2,1,0:T(8,128)(2,1)} %bitcast.34), custom_call_target="tpu_custom_call" | custom-call | flops 2000000000 | bytes 8388608 | tf_op jit(solution)/shard_map/attend/pallas_call | solution.py:322
  (53 shorter events, 14.5 us)
Async XLA Ops:
  7.2 13.9 %copy-start = (s32[16]{0:T(128)S(1)}, s32[16]{0:T(128)}, u32[]{:S(2)}) copy-start(s32[16]{0:T(128)} %param.15) | copy-start | bytes 196
  7.2 10.2 %copy-start.10 = (s32[3]{0:T(128)S(1)}, s32[3]{0:T(128)}, u32[]{:S(2)}) copy-start(s32[3]{0:T(128)} %param.14) | copy-start | bytes 40
  7.2 1.8 copy-start.3
  9.9 22.9 %all-to-all-start.2 = ((bf16[16,16,1152]{2,1,0:T(8,128)(2,1)}), bf16[16,16,1152]{2,1,0:T(8,128)(2,1)S(1)}, u32[]{:S(2)}, u32[]{:S(2)}) async-start(bf16[16,16,1152]{2,1,0:T(8,128)(2,1)} %get-tuple-element.19), calls=%async_computation.2 | async-start | bytes 1179648 | tf_op jit(solution)/shard_map/all_to_all | solution.py:371
  17.3 100.2 %copy-start.11 = (s32[3]{0:T(128)S(1)}, s32[3]{0:T(128)}, u32[]{:S(2)}) copy-start(s32[3]{0:T(128)} %param.13) | copy-start | bytes 40
  17.3 114.9 %all-gather.13.cloned.1.call-start = ((), (), s32[]{:S(2)}) async-start(), calls=%async_computation.5 | async-start | bytes 3760128 | tf_op jit(solution)/shard_map/all_gather | solution.py:397
  17.4 3.6 %collective-permute-start = (s32[3]{0:T(128)S(1)}, s32[3]{0:T(128)S(1)}, u32[]{:S(2)}, u32[]{:S(2)}) collective-permute-start(s32[3]{0:T(128)S(1)} %copy-done.10), channel_id=1, source_target_pairs={{0,16},{16,0},{1,17},{17,1},{2,18},{18,2},{3,19},{19,3},{4,20},{20... | collective-permute-start | bytes 44 | tf_op jit(solution)/shard_map/ppermute | solution.py:385
  21.1 111.1 %copy-start.1 = (bf16[128,4096]{1,0:T(8,128)(2,1)S(1)}, bf16[128,4096]{1,0:T(8,128)(2,1)}, u32[]{:S(2)}) copy-start(bf16[128,4096]{1,0:T(8,128)(2,1)} %hidden_ref.3) | copy-start | bytes 3145732
  21.1 111.1 %copy-start.6 = (bf16[128,512]{1,0:T(8,128)(2,1)S(1)}, bf16[128,512]{1,0:T(8,128)(2,1)}, u32[]{:S(2)}) copy-start(bf16[128,512]{1,0:T(8,128)(2,1)} %key_ref.1) | copy-start | bytes 393220
  21.1 111.1 %copy-start.7 = (bf16[128,512]{1,0:T(8,128)(2,1)S(1)}, bf16[128,512]{1,0:T(8,128)(2,1)}, u32[]{:S(2)}) copy-start(bf16[128,512]{1,0:T(8,128)(2,1)} %value_ref.1) | copy-start | bytes 393220
  32.9 0.8 copy-start.9
  42.2 5.3 %collective-permute-start.3 = (bf16[3,16,1152]{2,1,0:T(8,128)(2,1)}, bf16[3,16,1152]{2,1,0:T(8,128)(2,1)S(1)}, u32[]{:S(2)}, u32[]{:S(2)}) collective-permute-start(bf16[3,16,1152]{2,1,0:T(8,128)(2,1)} %get-tuple-element.21), channel_id=1, source_target_pairs={{0,16},{16,0},{1,17},{17,1},{2,18},{18,2},{3,19},{19,3},{4,20},{20... | collective-permute-start | bytes 331784 | tf_op jit(solution)/shard_map/ppermute | solution.py:393
  49.1 100.9 %all-gather.9.cloned.1.call-start = ((), (), s32[]{:S(2)}) async-start(), calls=%async_computation.3 | async-start | bytes 2506752 | tf_op jit(solution)/shard_map/all_gather | solution.py:397
  75.6 4.6 %collective-permute-start.1 = (bf16[3,16,768]{2,1,0:T(8,128)(2,1)}, bf16[3,16,768]{2,1,0:T(8,128)(2,1)S(1)}, u32[]{:S(2)}, u32[]{:S(2)}) collective-permute-start(bf16[3,16,768]{2,1,0:T(8,128)(2,1)} %get-tuple-element.15), channel_id=1, source_target_pairs={{0,16},{16,0},{1,17},{17,1},{2,18},{18,2},{3,19},{19,3},{4,20},{20... | collective-permute-start | bytes 221192 | tf_op jit(solution)/shard_map/ppermute | solution.py:393
  81.9 111.4 %all-gather.11.cloned.1.call-start = ((), (), s32[]{:S(2)}) async-start(), calls=%async_computation.4 | async-start | bytes 2506752 | tf_op jit(solution)/shard_map/all_gather | solution.py:397
  111.2 4.6 %collective-permute-start.2 = (bf16[3,16,768]{2,1,0:T(8,128)(2,1)}, bf16[3,16,768]{2,1,0:T(8,128)(2,1)S(1)}, u32[]{:S(2)}, u32[]{:S(2)}) collective-permute-start(bf16[3,16,768]{2,1,0:T(8,128)(2,1)} %get-tuple-element.18), channel_id=1, source_target_pairs={{0,16},{16,0},{1,17},{17,1},{2,18},{18,2},{3,19},{19,3},{4,20},{20... | collective-permute-start | bytes 221192 | tf_op jit(solution)/shard_map/ppermute | solution.py:393
  117.4 127.8 %all-gather.15.cloned.1.call-start = ((), (), s32[]{:S(2)}) async-start(), calls=%async_computation.6 | async-start | bytes 4456448 | tf_op jit(solution)/shard_map/all_gather | solution.py:405
  132.2 2.1 copy-start.2
  134.3 15.7 %copy-start.5 = (bf16[128,2048]{1,0:T(8,128)(2,1)S(1)}, bf16[128,2048]{1,0:T(8,128)(2,1)}, u32[]{:S(2)}) copy-start(bf16[128,2048]{1,0:T(8,128)(2,1)} %query_ref.1) | copy-start | bytes 1572868
  150.0 1.7 copy-start.4
  245.2 1.7 copy-start.8
Sparse Core Ops, SparseCore 0:
  49.2 57.3 all-gather.12
  109.5 40.4 all-gather.8
  152.2 40.9 all-gather.10
  195.9 49.3 all-gather.14
